TPU v7x, 32 devices: a whole 2x2x4 slice. The times are simulated.
32 devices in a mesh: domain: 8 (over z, x), band: 4 (over y, core).
Axes of the slice: x: 2, y: 2, z: 4, core: 2. Of those that a mesh axis runs over, the one named last changes fastest.
Arguments:
- orbitals: float32 [96, 48, 16, 128], P('band', 'domain'), may hold values from -8.8 to 8.8
- potential: float32 [48, 16, 128], P('domain', None, 'band'), may hold values from -1.5 to 0
Outputs:
- filtered: float32 [96, 48, 16, 128], P('band', 'domain')
- intersection: float32 [96, 96], P('band')
- hamiltonian: float32 [96, 96], P('band')
All inputs are finite; a program needn't handle non-finite values.
Results may differ from a plain program's by a relative error of at most 0.00005.
Values sent between devices are 32-bit elements; how exact they have to be, the bound alone decides.
A program may use at most 64 MiB of HBM per device.

v0:
```python
import jax
import jax.numpy as jnp
from jax import lax
from jax.sharding import PartitionSpec as P

DEGREE = 8


stencil_coeffs = (
    -5369.0 / 1800.0,
    12.0 / 7.0,
    -15.0 / 56.0,
    10.0 / 189.0,
    -1.0 / 112.0,
    2.0 / 1925.0,
    -1.0 / 16632.0,
)
stencil_reach = 6
lower_bound = 4.5
upper_bound = 15.5
lowest_bound = 1.0


def extended(cells, sides, width):
    for axis, dim in sides:
        count = lax.axis_size(axis)
        head = lax.slice_in_dim(cells, 0, width, axis=dim)
        tail = lax.slice_in_dim(cells, cells.shape[dim] - width, cells.shape[dim], axis=dim)
        cells = jnp.concatenate(
            [
                lax.ppermute(tail, axis, [(i, (i + 1) % count) for i in range(count)]),
                cells,
                lax.ppermute(head, axis, [((i + 1) % count, i) for i in range(count)]),
            ],
            axis=dim,
        )
    return cells


def laplace(grid_field):
    planes = grid_field.shape[1]
    size_y = grid_field.shape[2]
    size_z = grid_field.shape[3]
    padded_x = extended(grid_field, (("domain", 1),), 6)
    padded_yz = jnp.pad(
        grid_field, ((0, 0), (0, 0), (stencil_reach, stencil_reach), (stencil_reach, stencil_reach))
    )
    summed = 3.0 * stencil_coeffs[0] * grid_field
    for offset in range(1, stencil_reach + 1):
        along_x = (
            padded_x[:, stencil_reach + offset : stencil_reach + offset + planes]
            + padded_x[:, stencil_reach - offset : stencil_reach - offset + planes]
        )
        along_y = (
            padded_yz[
                :,
                :,
                stencil_reach + offset : stencil_reach + offset + size_y,
                stencil_reach : stencil_reach + size_z,
            ]
            + padded_yz[
                :,
                :,
                stencil_reach - offset : stencil_reach - offset + size_y,
                stencil_reach : stencil_reach + size_z,
            ]
        )
        along_z = (
            padded_yz[
                :,
                :,
                stencil_reach : stencil_reach + size_y,
                stencil_reach + offset : stencil_reach + offset + size_z,
            ]
            + padded_yz[
                :,
                :,
                stencil_reach : stencil_reach + size_y,
                stencil_reach - offset : stencil_reach - offset + size_z,
            ]
        )
        summed = summed + stencil_coeffs[offset] * (along_x + along_y + along_z)
    return summed


def apply_hamiltonian(grid_field, local_pot):
    return -0.5 * laplace(grid_field) + local_pot[None] * grid_field


def contract(left, right):
    return lax.dot_general(
        left,
        right,
        (((1,), (1,)), ((), ())),
        precision=lax.Precision.HIGHEST,
        preferred_element_type=jnp.float32,
    )


def body(orbitals, potential):
    local_pot = lax.all_gather(potential, "band", axis=2, tiled=True)
    half_width = (upper_bound - lower_bound) / 2.0
    centre = (upper_bound + lower_bound) / 2.0
    sigma_first = half_width / (lowest_bound - centre)
    previous = orbitals
    current = (apply_hamiltonian(previous, local_pot) - centre * previous) * (
        sigma_first / half_width
    )
    sigma_now = sigma_first
    for degree_step in range(2, DEGREE + 1):
        sigma_next = 1.0 / (2.0 / sigma_first - sigma_now)
        update = (apply_hamiltonian(current, local_pot) - centre * current) * (
            2.0 * sigma_next / half_width
        ) - sigma_now * sigma_next * previous
        previous = current
        current = update
        sigma_now = sigma_next
    h_image = apply_hamiltonian(current, local_pot)
    orb_dev = current.shape[0]
    cell_count = current.shape[1] * current.shape[2] * current.shape[3] * lax.axis_size("domain")
    flat_panel = current.reshape(orb_dev, -1)
    flat_image = h_image.reshape(orb_dev, -1)
    panel_in = lax.all_gather(flat_panel, "band", axis=0, tiled=True)
    s_part = contract(flat_panel, panel_in)
    h_part = contract(flat_image, panel_in)
    s_total, h_total = lax.psum((s_part, h_part), "domain")
    intersection = s_total / cell_count
    hamiltonian = h_total / cell_count
    return (current, intersection, hamiltonian)


def solution(mesh):
    placed = (P("band", "domain", None, None), P("domain", None, "band"))
    return jax.shard_map(
        body,
        mesh=mesh,
        in_specs=placed,
        out_specs=(P("band", "domain", None, None), P("band", None), P("band", None)),
        check_vma=False,
    )
```

profile of v0, /device:TPU:0, one launch (start us, length us, event | category | flops | bytes accessed | tf_op | source)
XLA Modules:
  0.0 601.9 jit_solution(9702652618128940189)
XLA Ops:
  7.2 0.0 all-gather.2.cloned.1.call-start
  7.2 3.0 collective-permute-start.1
  10.2 3.1 collective-permute-start
  13.3 0.9 copy.8
  14.2 7.3 %all_gather.6 = f32[6,16,128]{1,0,2:T(8,128)S(1)} all-gather(f32[6,16,32]{1,0,2:T(8,128)S(1)} %copy.8), channel_id=1, replica_groups=mesh['domain'=8,'band'=4] {'band'}, dimensions={2}, use_global_device_ids=true | all-gather | bytes 61440 | tf_op jit(solution)/shard_map/all_gather | solution.py:101
  21.5 0.8 copy.9
  22.3 38.7 %collective-permute-done.1 = f32[24,6,16,128]{3,2,1,0:T(8,128)S(1)} collective-permute-done((f32[24,6,16,128]{3,2,1,0:T(8,128)}, f32[24,6,16,128]{3,2,1,0:T(8,128)S(1)}, u32[]{:S(2)}, u32[]{:S(2)}) %collective-permute-start.1) | collective-permute-done | bytes 1179680 | tf_op jit(solution)/shard_map/ppermute | solution.py:31
  61.0 1.0 copy-done.6
  62.0 0.1 constant_dynamic-update-slice_fusion.3
  62.1 0.0 copy-done.3
  62.1 0.2 constant_dynamic-update-slice_fusion.1
  62.3 0.9 collective-permute-done
  63.2 1.4 constant_dynamic-update-slice_fusion
  64.6 7.4 %broadcast_multiply_fusion = (f32[24,6,16,128]{3,2,1,0:T(8,128)}, f32[24,6,16,128]{3,2,1,0:T(8,128)}) fusion(f32[24,6,16,128]{3,2,1,0:T(8,128)S(1)} %copy-done.3, f32[6,16,128]{2,1,0:T(8,128)} %copy.9, f32[24,6,16,128]{3,2,1,0:T(8,128)} %collective-permute-done, f32[24,6,16,128]{3,2,1,0:T(8,128)} %copy-done.6, f32[24,12,16,128]{3,2,1,0:T(8,128)} %copy-done, ...), kind=kLoop, calls=%fused_computation.837 | loop fusion | flops 14450688 | bytes 17743872 | tf_op jit(solution)/shard_map/mul | solution.py:106
  72.0 5.4 collective-permute-start.2
  77.4 0.0 collective-permute-start.3
  77.4 0.8 broadcast_multiply_fusion.1
  78.2 46.7 %collective-permute-done.2 = f32[24,6,16,128]{3,2,1,0:T(8,128)S(1)} collective-permute-done((f32[24,6,16,128]{3,2,1,0:T(8,128)}, f32[24,6,16,128]{3,2,1,0:T(8,128)S(1)}, u32[]{:S(2)}, u32[]{:S(2)}) %collective-permute-start.2) | collective-permute-done | bytes 1179680 | tf_op jit(solution)/shard_map/ppermute | solution.py:33
  124.9 0.3 collective-permute-done.3
  125.2 20.6 %fusion.254 = f32[24,6,16,128]{3,2,1,0:T(8,128)S(1)} fusion(f32[24,6,16,128]{3,2,1,0:T(8,128)S(1)} %collective-permute-done.3, f32[24,6,16,128]{3,2,1,0:T(8,128)} %get-tuple-element.5, f32[24,6,16,128]{3,2,1,0:T(8,128)S(1)} %collective-permute-done.2, f32[24,6,16,128]{3,2,1,0:T(8,128)S(1)} %copy-done.3, f32[24,6,16,128]{3,2,1,0:T(8,128)} %get-tuple-element.6, ...), kind=kLoop, calls=%fused_computation.598 | loop fusion | flops 17989632 | bytes 7127040 | tf_op jit(solution)/shard_map/sub | solution.py:112
  145.8 4.7 collective-permute-start.4
  150.5 0.0 collective-permute-start.5
  150.5 49.1 %collective-permute-done.4 = f32[24,6,16,128]{3,2,1,0:T(8,128)S(1)} collective-permute-done((f32[24,6,16,128]{3,2,1,0:T(8,128)S(1)}, f32[24,6,16,128]{3,2,1,0:T(8,128)S(1)}, u32[]{:S(2)}, u32[]{:S(2)}) %collective-permute-start.4) | collective-permute-done | bytes 1179680 | tf_op jit(solution)/shard_map/ppermute | solution.py:33
  199.7 0.0 collective-permute-done.5
  199.7 4.0 fusion.219
  203.7 3.1 collective-permute-start.6
  206.8 0.0 collective-permute-start.7
  206.8 49.9 %collective-permute-done.6 = f32[24,6,16,128]{3,2,1,0:T(8,128)S(1)} collective-permute-done((f32[24,6,16,128]{3,2,1,0:T(8,128)S(1)}, f32[24,6,16,128]{3,2,1,0:T(8,128)S(1)}, u32[]{:S(2)}, u32[]{:S(2)}) %collective-permute-start.6) | collective-permute-done | bytes 1179680 | tf_op jit(solution)/shard_map/ppermute | solution.py:33
  256.7 0.0 collective-permute-done.7
  256.7 4.0 fusion.184
  260.7 2.5 collective-permute-start.8
  263.2 0.0 collective-permute-start.9
  263.2 49.9 %collective-permute-done.8 = f32[24,6,16,128]{3,2,1,0:T(8,128)S(1)} collective-permute-done((f32[24,6,16,128]{3,2,1,0:T(8,128)S(1)}, f32[24,6,16,128]{3,2,1,0:T(8,128)S(1)}, u32[]{:S(2)}, u32[]{:S(2)}) %collective-permute-start.8) | collective-permute-done | bytes 1179680 | tf_op jit(solution)/shard_map/ppermute | solution.py:33
  313.1 0.0 collective-permute-done.9
  313.1 4.0 fusion.149
  317.1 4.2 collective-permute-start.10
  321.3 0.0 collective-permute-start.11
  321.3 48.2 %collective-permute-done.10 = f32[24,6,16,128]{3,2,1,0:T(8,128)S(1)} collective-permute-done((f32[24,6,16,128]{3,2,1,0:T(8,128)S(1)}, f32[24,6,16,128]{3,2,1,0:T(8,128)S(1)}, u32[]{:S(2)}, u32[]{:S(2)}) %collective-permute-start.10) | collective-permute-done | bytes 1179680 | tf_op jit(solution)/shard_map/ppermute | solution.py:33
  369.5 0.2 collective-permute-done.11
  369.7 4.0 fusion.114
  373.6 5.0 collective-permute-start.12
  378.6 0.0 collective-permute-start.13
  378.6 49.0 %collective-permute-done.12 = f32[24,6,16,128]{3,2,1,0:T(8,128)S(1)} collective-permute-done((f32[24,6,16,128]{3,2,1,0:T(8,128)S(1)}, f32[24,6,16,128]{3,2,1,0:T(8,128)S(1)}, u32[]{:S(2)}, u32[]{:S(2)}) %collective-permute-start.12) | collective-permute-done | bytes 1179680 | tf_op jit(solution)/shard_map/ppermute | solution.py:33
  427.6 0.2 collective-permute-done.13
  427.8 4.0 fusion.79
  431.8 3.5 collective-permute-start.14
  435.3 0.0 collective-permute-start.15
  435.3 50.5 %collective-permute-done.14 = f32[24,6,16,128]{3,2,1,0:T(8,128)S(1)} collective-permute-done((f32[24,6,16,128]{3,2,1,0:T(8,128)S(1)}, f32[24,6,16,128]{3,2,1,0:T(8,128)S(1)}, u32[]{:S(2)}, u32[]{:S(2)}) %collective-permute-start.14) | collective-permute-done | bytes 1179680 | tf_op jit(solution)/shard_map/ppermute | solution.py:33
  485.7 0.0 collective-permute-done.15
  485.7 4.0 fusion.44
  489.7 0.0 copy-start.2
  489.7 1.7 copy.19
  491.5 0.0 all-gather.2.cloned.1.call-update
  491.5 2.0 collective-permute-start.16
  493.5 0.0 collective-permute-start.17
  493.6 50.6 %collective-permute-done.16 = f32[24,6,16,128]{3,2,1,0:T(8,128)S(1)} collective-permute-done((f32[24,6,16,128]{3,2,1,0:T(8,128)S(1)}, f32[24,6,16,128]{3,2,1,0:T(8,128)S(1)}, u32[]{:S(2)}, u32[]{:S(2)}) %collective-permute-start.16) | collective-permute-done | bytes 1179680 | tf_op jit(solution)/shard_map/ppermute | solution.py:33
  544.2 0.0 collective-permute-done.17
  544.2 4.0 fusion.9
  548.2 0.0 all-gather.2.cloned.1.call-done
  548.2 6.1 %fusion.471 = f32[24,96]{1,0:T(8,128)S(1)} fusion(f32[96,12288]{1,0:T(8,128)} %all-gather.2.cloned.1.call-done, f32[3,8,96,128]{3,2,1,0:T(8,128)S(1)} %bitcast.14), kind=kOutput, calls=%fused_computation.845 | convolution fusion | flops 339738624 | bytes 5907456 | tf_op jit(solution)/shard_map/dot_general | solution.py:91
  554.3 0.0 copy-done.1
  554.3 3.9 fusion.460
  558.1 36.3 %all-reduce.9 = (f32[24,96]{1,0:T(8,128)S(1)}, f32[24,96]{1,0:T(8,128)S(1)}) all-reduce(f32[24,96]{1,0:T(8,128)S(1)} %fusion.471, f32[24,96]{1,0:T(8,128)S(1)} %fusion.460), channel_id=1, replica_groups=mesh['domain'=8,'band'=4] {'domain'}, use_global_device_ids=true, to_apply=%region_0.1 | all-reduce | flops 4608 | bytes 36864 | tf_op jit(solution)/shard_map/psum | solution.py:126
  594.4 0.6 broadcast_multiply_fusion.2
  (10 shorter events, 0.0 us)
Async XLA Ops:
  7.2 541.0 %all-gather.2.cloned.1.call-start = ((), (), s32[]{:S(2)}) async-start(), calls=%async_computation | async-start | bytes 5898240 | tf_op jit(solution)/shard_map/all_gather | solution.py:123
  7.2 53.8 %collective-permute-start.1 = (f32[24,6,16,128]{3,2,1,0:T(8,128)}, f32[24,6,16,128]{3,2,1,0:T(8,128)S(1)}, u32[]{:S(2)}, u32[]{:S(2)}) collective-permute-start(f32[24,6,16,128]{3,2,1,0:T(8,128)} %param.2), channel_id=1, source_target_pairs={{0,4},{4,8},{8,12},{12,16},{16,20},{20,24},{24,28},{28,0},{1,5},{5... | collective-permute-start | bytes 3538952 | tf_op jit(solution)/shard_map/ppermute | solution.py:31
  10.2 53.0 %collective-permute-start = (f32[24,6,16,128]{3,2,1,0:T(8,128)}, f32[24,6,16,128]{3,2,1,0:T(8,128)}, u32[]{:S(2)}, u32[]{:S(2)}) collective-permute-start(f32[24,6,16,128]{3,2,1,0:T(8,128)} %param.2), channel_id=1, source_target_pairs={{4,0},{8,4},{12,8},{16,12},{20,16},{24,20},{28,24},{0,28},{5,1},{9... | collective-permute-start | bytes 3538952 | tf_op jit(solution)/shard_map/ppermute | solution.py:33
  22.3 39.8 %copy-start.3 = (f32[24,6,16,128]{3,2,1,0:T(8,128)S(1)}, f32[24,6,16,128]{3,2,1,0:T(8,128)}, u32[]{:S(2)}) copy-start(f32[24,6,16,128]{3,2,1,0:T(8,128)} %param.2) | copy-start | bytes 3538948
  61.0 1.0 copy-start.6
  62.3 2.3 copy-start
  72.0 52.9 %collective-permute-start.2 = (f32[24,6,16,128]{3,2,1,0:T(8,128)}, f32[24,6,16,128]{3,2,1,0:T(8,128)S(1)}, u32[]{:S(2)}, u32[]{:S(2)}) collective-permute-start(f32[24,6,16,128]{3,2,1,0:T(8,128)} %get-tuple-element.5), channel_id=1, source_target_pairs={{4,0},{8,4},{12,8},{16,12},{20,16},{24,20},{28,24},{0,28},{5,1},{9... | collective-permute-start | bytes 3538952 | tf_op jit(solution)/shard_map/ppermute | solution.py:33
  77.4 47.8 %collective-permute-start.3 = (f32[24,6,16,128]{3,2,1,0:T(8,128)}, f32[24,6,16,128]{3,2,1,0:T(8,128)S(1)}, u32[]{:S(2)}, u32[]{:S(2)}) collective-permute-start(f32[24,6,16,128]{3,2,1,0:T(8,128)} %get-tuple-element.5), channel_id=1, source_target_pairs={{0,4},{4,8},{8,12},{12,16},{16,20},{20,24},{24,28},{28,0},{1,5},{5... | collective-permute-start | bytes 3538952 | tf_op jit(solution)/shard_map/ppermute | solution.py:31
  125.2 74.5 %copy-start.4 = (f32[24,6,16,128]{3,2,1,0:T(8,128)S(1)}, f32[24,6,16,128]{3,2,1,0:T(8,128)}, u32[]{:S(2)}) copy-start(f32[24,6,16,128]{3,2,1,0:T(8,128)} %get-tuple-element.6) | copy-start | bytes 3538948
  125.2 74.5 %copy-start.5 = (f32[6,16,128]{2,1,0:T(8,128)S(1)}, f32[6,16,128]{2,1,0:T(8,128)}, u32[]{:S(2)}) copy-start(f32[6,16,128]{2,1,0:T(8,128)} %copy.9) | copy-start | bytes 147460
  145.8 53.9 %collective-permute-start.4 = (f32[24,6,16,128]{3,2,1,0:T(8,128)S(1)}, f32[24,6,16,128]{3,2,1,0:T(8,128)S(1)}, u32[]{:S(2)}, u32[]{:S(2)}) collective-permute-start(f32[24,6,16,128]{3,2,1,0:T(8,128)S(1)} %fusion.254), channel_id=1, source_target_pairs={{4,0},{8,4},{12,8},{16,12},{20,16},{24,20},{28,24},{0,28},{5,1},{9... | collective-permute-start | bytes 3538952 | tf_op jit(solution)/shard_map/ppermute | solution.py:33
  150.5 49.1 %collective-permute-start.5 = (f32[24,6,16,128]{3,2,1,0:T(8,128)S(1)}, f32[24,6,16,128]{3,2,1,0:T(8,128)S(1)}, u32[]{:S(2)}, u32[]{:S(2)}) collective-permute-start(f32[24,6,16,128]{3,2,1,0:T(8,128)S(1)} %fusion.254), channel_id=1, source_target_pairs={{0,4},{4,8},{8,12},{12,16},{16,20},{20,24},{24,28},{28,0},{1,5},{5... | collective-permute-start | bytes 3538952 | tf_op jit(solution)/shard_map/ppermute | solution.py:31
  203.7 53.0 %collective-permute-start.6 = (f32[24,6,16,128]{3,2,1,0:T(8,128)S(1)}, f32[24,6,16,128]{3,2,1,0:T(8,128)S(1)}, u32[]{:S(2)}, u32[]{:S(2)}) collective-permute-start(f32[24,6,16,128]{3,2,1,0:T(8,128)S(1)} %fusion.219), channel_id=1, source_target_pairs={{4,0},{8,4},{12,8},{16,12},{20,16},{24,20},{28,24},{0,28},{5,1},{9... | collective-permute-start | bytes 3538952 | tf_op jit(solution)/shard_map/ppermute | solution.py:33
  206.8 49.9 %collective-permute-start.7 = (f32[24,6,16,128]{3,2,1,0:T(8,128)S(1)}, f32[24,6,16,128]{3,2,1,0:T(8,128)S(1)}, u32[]{:S(2)}, u32[]{:S(2)}) collective-permute-start(f32[24,6,16,128]{3,2,1,0:T(8,128)S(1)} %fusion.219), channel_id=1, source_target_pairs={{0,4},{4,8},{8,12},{12,16},{16,20},{20,24},{24,28},{28,0},{1,5},{5... | collective-permute-start | bytes 3538952 | tf_op jit(solution)/shard_map/ppermute | solution.py:31
  260.7 52.4 %collective-permute-start.8 = (f32[24,6,16,128]{3,2,1,0:T(8,128)S(1)}, f32[24,6,16,128]{3,2,1,0:T(8,128)S(1)}, u32[]{:S(2)}, u32[]{:S(2)}) collective-permute-start(f32[24,6,16,128]{3,2,1,0:T(8,128)S(1)} %fusion.184), channel_id=1, source_target_pairs={{4,0},{8,4},{12,8},{16,12},{20,16},{24,20},{28,24},{0,28},{5,1},{9... | collective-permute-start | bytes 3538952 | tf_op jit(solution)/shard_map/ppermute | solution.py:33
  263.2 49.9 %collective-permute-start.9 = (f32[24,6,16,128]{3,2,1,0:T(8,128)S(1)}, f32[24,6,16,128]{3,2,1,0:T(8,128)S(1)}, u32[]{:S(2)}, u32[]{:S(2)}) collective-permute-start(f32[24,6,16,128]{3,2,1,0:T(8,128)S(1)} %fusion.184), channel_id=1, source_target_pairs={{0,4},{4,8},{8,12},{12,16},{16,20},{20,24},{24,28},{28,0},{1,5},{5... | collective-permute-start | bytes 3538952 | tf_op jit(solution)/shard_map/ppermute | solution.py:31
  317.1 52.4 %collective-permute-start.10 = (f32[24,6,16,128]{3,2,1,0:T(8,128)S(1)}, f32[24,6,16,128]{3,2,1,0:T(8,128)S(1)}, u32[]{:S(2)}, u32[]{:S(2)}) collective-permute-start(f32[24,6,16,128]{3,2,1,0:T(8,128)S(1)} %fusion.149), channel_id=1, source_target_pairs={{4,0},{8,4},{12,8},{16,12},{20,16},{24,20},{28,24},{0,28},{5,1},{9... | collective-permute-start | bytes 3538952 | tf_op jit(solution)/shard_map/ppermute | solution.py:33
  321.3 48.3 %collective-permute-start.11 = (f32[24,6,16,128]{3,2,1,0:T(8,128)S(1)}, f32[24,6,16,128]{3,2,1,0:T(8,128)S(1)}, u32[]{:S(2)}, u32[]{:S(2)}) collective-permute-start(f32[24,6,16,128]{3,2,1,0:T(8,128)S(1)} %fusion.149), channel_id=1, source_target_pairs={{0,4},{4,8},{8,12},{12,16},{16,20},{20,24},{24,28},{28,0},{1,5},{5... | collective-permute-start | bytes 3538952 | tf_op jit(solution)/shard_map/ppermute | solution.py:31
  373.6 54.0 %collective-permute-start.12 = (f32[24,6,16,128]{3,2,1,0:T(8,128)S(1)}, f32[24,6,16,128]{3,2,1,0:T(8,128)S(1)}, u32[]{:S(2)}, u32[]{:S(2)}) collective-permute-start(f32[24,6,16,128]{3,2,1,0:T(8,128)S(1)} %fusion.114), channel_id=1, source_target_pairs={{4,0},{8,4},{12,8},{16,12},{20,16},{24,20},{28,24},{0,28},{5,1},{9... | collective-permute-start | bytes 3538952 | tf_op jit(solution)/shard_map/ppermute | solution.py:33
  378.6 49.1 %collective-permute-start.13 = (f32[24,6,16,128]{3,2,1,0:T(8,128)S(1)}, f32[24,6,16,128]{3,2,1,0:T(8,128)S(1)}, u32[]{:S(2)}, u32[]{:S(2)}) collective-permute-start(f32[24,6,16,128]{3,2,1,0:T(8,128)S(1)} %fusion.114), channel_id=1, source_target_pairs={{0,4},{4,8},{8,12},{12,16},{16,20},{20,24},{24,28},{28,0},{1,5},{5... | collective-permute-start | bytes 3538952 | tf_op jit(solution)/shard_map/ppermute | solution.py:31
  431.8 54.0 %collective-permute-start.14 = (f32[24,6,16,128]{3,2,1,0:T(8,128)S(1)}, f32[24,6,16,128]{3,2,1,0:T(8,128)S(1)}, u32[]{:S(2)}, u32[]{:S(2)}) collective-permute-start(f32[24,6,16,128]{3,2,1,0:T(8,128)S(1)} %fusion.79), channel_id=1, source_target_pairs={{4,0},{8,4},{12,8},{16,12},{20,16},{24,20},{28,24},{0,28},{5,1},{9... | collective-permute-start | bytes 3538952 | tf_op jit(solution)/shard_map/ppermute | solution.py:33
  435.3 50.5 %collective-permute-start.15 = (f32[24,6,16,128]{3,2,1,0:T(8,128)S(1)}, f32[24,6,16,128]{3,2,1,0:T(8,128)S(1)}, u32[]{:S(2)}, u32[]{:S(2)}) collective-permute-start(f32[24,6,16,128]{3,2,1,0:T(8,128)S(1)} %fusion.79), channel_id=1, source_target_pairs={{0,4},{4,8},{8,12},{12,16},{16,20},{20,24},{24,28},{28,0},{1,5},{5... | collective-permute-start | bytes 3538952 | tf_op jit(solution)/shard_map/ppermute | solution.py:31
  489.7 58.5 %copy-start.2 = (f32[24,6,16,128]{3,2,1,0:T(8,128)}, f32[24,6,16,128]{3,2,1,0:T(8,128)S(1)}, u32[]{:S(2)}) copy-start(f32[24,6,16,128]{3,2,1,0:T(8,128)S(1)} %fusion.44) | copy-start | bytes 3538948
  491.5 52.7 %collective-permute-start.16 = (f32[24,6,16,128]{3,2,1,0:T(8,128)S(1)}, f32[24,6,16,128]{3,2,1,0:T(8,128)S(1)}, u32[]{:S(2)}, u32[]{:S(2)}) collective-permute-start(f32[24,6,16,128]{3,2,1,0:T(8,128)S(1)} %fusion.44), channel_id=1, source_target_pairs={{4,0},{8,4},{12,8},{16,12},{20,16},{24,20},{28,24},{0,28},{5,1},{9... | collective-permute-start | bytes 3538952 | tf_op jit(solution)/shard_map/ppermute | solution.py:33
  493.5 50.7 %collective-permute-start.17 = (f32[24,6,16,128]{3,2,1,0:T(8,128)S(1)}, f32[24,6,16,128]{3,2,1,0:T(8,128)S(1)}, u32[]{:S(2)}, u32[]{:S(2)}) collective-permute-start(f32[24,6,16,128]{3,2,1,0:T(8,128)S(1)} %fusion.44), channel_id=1, source_target_pairs={{0,4},{4,8},{8,12},{12,16},{16,20},{20,24},{24,28},{28,0},{1,5},{5... | collective-permute-start | bytes 3538952 | tf_op jit(solution)/shard_map/ppermute | solution.py:31
  548.2 6.1 %copy-start.1 = (f32[96,12288]{1,0:T(8,128)S(1)}, f32[96,12288]{1,0:T(8,128)}, u32[]{:S(2)}) copy-start(f32[96,12288]{1,0:T(8,128)} %all-gather.2.cloned.1.call-done) | copy-start | bytes 14155780
Sparse Core Ops, SparseCore 0:
  491.6 36.2 all-gather.1
where the time goes:
time: 602 us
  waiting for transfers between devices  434 us (72%)
  other arithmetic  57.3 us (10%)
  blocking collectives  43.6 us (7%)
  starting transfers between devices  36.6 us (6%)
  between operations  14.2 us (2%)
  matrix products  9.91 us (2%)
  local copies, waits for them, and re-layouts  6.09 us (1%)
    ppermute x9, waiting for transfers between devices, extended(): lax.ppermute(head, axis, [((i + 1) % count, i) for i in range(count)])  395 us
    sub x7, other arithmetic, body(): (apply_hamiltonian(current, local_pot) - centre * current) * (2.0 * sigma...  44.5 us
    ppermute x9, waiting for transfers between devices, extended(): lax.ppermute(tail, axis, [(i, (i + 1) % count) for i in range(count)])  39.3 us
    psum x1, blocking collectives, body(): s_total, h_total = lax.psum((s_part, h_part), 'domain')  36.3 us
    ppermute x9, starting transfers between devices, extended(): lax.ppermute(head, axis, [((i + 1) % count, i) for i in range(count)])  33.5 us
  transfers between devices with their start and end apart: 19, of which 13 were waited for; matrix products, arithmetic and copies ran while one was open for 1% of the time, Pallas kernels for 0%

commit v1 on v0

--- a/solution.py
+++ b/solution.py
@@ -1,7 +1,13 @@
+import functools
+
 import jax
 import jax.numpy as jnp
 from jax import lax
+from jax.experimental import pallas as pl
+from jax.experimental.pallas import tpu as pltpu
 from jax.sharding import PartitionSpec as P
+import ml_dtypes
+import numpy as np
 
 DEGREE = 8
 
@@ -97,7 +103,7 @@
     )
 
 
-def body(orbitals, potential):
+def body_by_block(orbitals, potential):
     local_pot = lax.all_gather(potential, "band", axis=2, tiled=True)
     half_width = (upper_bound - lower_bound) / 2.0
     centre = (upper_bound + lower_bound) / 2.0
@@ -129,6 +135,324 @@
     return (current, intersection, hamiltonian)
 
 
+pad_rows = 8
+
+
+def schedule():
+    half_width = (upper_bound - lower_bound) / 2.0
+    centre = (upper_bound + lower_bound) / 2.0
+    sigma_first = half_width / (lowest_bound - centre)
+    steps = [(sigma_first / half_width, 0.0)]
+    sigma_now = sigma_first
+    for degree_step in range(2, DEGREE + 1):
+        sigma_next = 1.0 / (2.0 / sigma_first - sigma_now)
+        steps.append((2.0 * sigma_next / half_width, sigma_now * sigma_next))
+        sigma_now = sigma_next
+    return centre, steps
+
+
+def band_matrix(size):
+    full = np.zeros((size, size), np.float64)
+    for offset in range(1, stencil_reach + 1):
+        full += -0.5 * stencil_coeffs[offset] * (np.eye(size, k=offset) + np.eye(size, k=-offset))
+    terms = []
+    for _ in range(3):
+        terms.append(full.astype(ml_dtypes.bfloat16))
+        full = full - terms[-1].astype(np.float64)
+    upper = np.concatenate(terms, axis=1)
+    lower = np.concatenate([terms[0], terms[1], np.zeros_like(terms[2])], axis=1)
+    return np.concatenate([upper, lower], axis=0)
+
+
+def shifted_h(src, group, groups, shifted_pot, weights):
+    reach = stencil_reach
+    size_y = src.shape[1] - 2 * pad_rows
+    size_z = src.shape[2]
+    before = lax.rem(group + groups - 1, groups) * reach
+    here = group * reach
+    after = lax.rem(group + 1, groups) * reach
+
+    def plane(index, shift=0):
+        if index < 0:
+            base = before + reach + index
+        elif index < reach:
+            base = here + index
+        else:
+            base = after + index - reach
+        return src[base, pl.ds(pad_rows + shift, size_y), :]
+
+    center = [plane(i) for i in range(reach)]
+    cells = jnp.concatenate(center, axis=0)
+    high = cells.astype(jnp.bfloat16)
+    low = (cells - high.astype(jnp.float32)).astype(jnp.bfloat16)
+    along_z = jnp.dot(
+        jnp.concatenate([high, low], axis=1), weights, preferred_element_type=jnp.float32
+    )
+    along_z = along_z[:, :size_z] + (along_z[:, size_z : 2 * size_z] + along_z[:, 2 * size_z :])
+    planes = {i: plane(i) for i in range(-reach, 0)}
+    planes.update({i: center[i] for i in range(reach)})
+    planes.update({i: plane(i) for i in range(reach, 2 * reach)})
+    results = []
+    for i in range(reach):
+        total = shifted_pot[here + i] * center[i] + along_z[i * size_y : (i + 1) * size_y]
+        for offset in range(1, reach + 1):
+            pairs = (planes[i + offset] + planes[i - offset]) + (plane(i, offset) + plane(i, -offset))
+            total = total + (-0.5 * stencil_coeffs[offset]) * pairs
+        results.append(total)
+    return results
+
+
+def filter_kernel(orb_ref, pot_ref, weight_ref, out_ref, image_ref, first, second, shifted_pot):
+    count, size_x, size_y, size_z = orb_ref.shape
+    reach = stencil_reach
+    groups = size_x // reach
+    centre, steps = schedule()
+    weights = weight_ref[...]
+    shifted_pot[...] = pot_ref[...] + (-1.5 * stencil_coeffs[0] - centre)
+    zeros = jnp.zeros((size_x, pad_rows, size_z), jnp.float32)
+    for buf in (first, second):
+        buf[:, pl.ds(0, pad_rows), :] = zeros
+        buf[:, pl.ds(pad_rows + size_y, pad_rows), :] = zeros
+    inner = pl.ds(pad_rows, size_y)
+
+    def one_orbital(orb, carry):
+        first[:, inner, :] = orb_ref[orb]
+        buffers = [first, second]
+        for scale, back in steps:
+            src, dst = buffers
+
+            def one_group(group, carry, src=src, dst=dst, scale=scale, back=back):
+                for i, total in enumerate(shifted_h(src, group, groups, shifted_pot, weights)):
+                    update = total * scale
+                    if back:
+                        update = update - back * dst[group * reach + i, inner, :]
+                    dst[group * reach + i, inner, :] = update
+                return carry
+
+            lax.fori_loop(0, groups, one_group, 0)
+            buffers = [dst, src]
+        src = buffers[0]
+
+        def image_group(group, carry):
+            for i, total in enumerate(shifted_h(src, group, groups, shifted_pot, weights)):
+                cells = src[group * reach + i, inner, :]
+                out_ref[orb, group * reach + i] = cells
+                image_ref[orb, group * reach + i] = total + centre * cells
+            return carry
+
+        lax.fori_loop(0, groups, image_group, 0)
+        return carry
+
+    lax.fori_loop(0, count, one_orbital, 0)
+
+
+def filter_orbitals(orbitals, potential):
+    count, size_x, size_y, size_z = orbitals.shape
+    vmem = pl.BlockSpec(memory_space=pltpu.VMEM)
+    padded = pltpu.VMEM((size_x, size_y + 2 * pad_rows, size_z), jnp.float32)
+    return pl.pallas_call(
+        filter_kernel,
+        out_shape=[jax.ShapeDtypeStruct(orbitals.shape, jnp.float32)] * 2,
+        in_specs=[vmem] * 3,
+        out_specs=[vmem] * 2,
+        scratch_shapes=[padded, padded, pltpu.VMEM((size_x, size_y, size_z), jnp.float32)],
+        compiler_params=pltpu.CompilerParams(vmem_limit_bytes=32 * 1024 * 1024),
+    )(orbitals, potential, jnp.asarray(band_matrix(size_z)))
+
+
+def greet(peers):
+    barrier = pltpu.get_barrier_semaphore()
+    for peer in peers:
+        pl.semaphore_signal(barrier, inc=1, device_id=peer, device_id_type=pl.DeviceIdType.MESH)
+    pl.semaphore_wait(barrier, len(peers))
+
+
+def others(axis, count):
+    me = lax.axis_index(axis)
+    return [{axis: lax.rem(me + step, count)} for step in range(1, count)]
+
+
+def send(src, dst, send_sem, recv_sem, peer):
+    copy = pltpu.make_async_remote_copy(
+        src_ref=src,
+        dst_ref=dst,
+        send_sem=send_sem,
+        recv_sem=recv_sem,
+        device_id=peer,
+        device_id_type=pl.DeviceIdType.MESH,
+    )
+    copy.start()
+    return copy
+
+
+def potential_kernel(domains, bands, part_ref, out_ref, by_band, whole, band_sems, domain_sems):
+    planes, size_y, part = part_ref.shape
+    band, domain = lax.axis_index("band"), lax.axis_index("domain")
+    band_peers, domain_peers = others("band", bands), others("domain", domains)
+    greet(band_peers + domain_peers)
+    spread = jnp.concatenate([part_ref[...]] * bands, axis=2)
+    lane = lax.broadcasted_iota(jnp.int32, spread.shape, 2)
+    mine = (lane >= band * part) & (lane < (band + 1) * part)
+    by_band[band] = jnp.where(mine, spread, 0.0)
+    copies = [
+        send(by_band.at[band], by_band.at[band], band_sems.at[0, i], band_sems.at[1, i], peer)
+        for i, peer in enumerate(band_peers)
+    ]
+    for copy in copies:
+        copy.wait()
+    total = by_band[0]
+    for i in range(1, bands):
+        total = total + by_band[i]
+    block = pl.ds(domain * planes, planes)
+    whole[block] = total
+    copies = [
+        send(whole.at[block], whole.at[block], domain_sems.at[0, i], domain_sems.at[1, i], peer)
+        for i, peer in enumerate(domain_peers)
+    ]
+    for copy in copies:
+        copy.wait()
+    out_ref[...] = whole[...]
+
+
+def whole_potential(potential):
+    domains, bands = lax.axis_size("domain"), lax.axis_size("band")
+    planes, size_y, part = potential.shape
+    vmem = pl.BlockSpec(memory_space=pltpu.VMEM)
+    whole = (domains * planes, size_y, bands * part)
+    return pl.pallas_call(
+        functools.partial(potential_kernel, domains, bands),
+        out_shape=jax.ShapeDtypeStruct(whole, jnp.float32),
+        in_specs=[vmem],
+        out_specs=vmem,
+        scratch_shapes=[
+            pltpu.VMEM((bands, planes, size_y, bands * part), jnp.float32),
+            pltpu.VMEM(whole, jnp.float32),
+            pltpu.SemaphoreType.DMA((2, bands - 1)),
+            pltpu.SemaphoreType.DMA((2, domains - 1)),
+        ],
+        compiler_params=pltpu.CompilerParams(collective_id=0, has_side_effects=True),
+    )(potential)
+
+
+def tiles_kernel(
+    domains, bands, cell_count, field_ref, image_ref, s_ref, h_ref,
+    field, image, rows_out, rows_in, part, parts, field_sems, image_sems, own_sems, row_sems, part_sems,
+):
+    orb_dev, rows, lanes = field_ref.shape
+    share = rows // bands
+    orbs = orb_dev * bands
+    band, domain = lax.axis_index("band"), lax.axis_index("domain")
+    band_peers, domain_peers = others("band", bands), others("domain", domains)
+    greet(band_peers + domain_peers)
+    mine = pl.ds(pl.multiple_of(band * orb_dev, orb_dev), orb_dev)
+    copies = []
+    for src, dst, sems in ((field_ref, field, field_sems), (image_ref, image, image_sems)):
+        for i, peer in enumerate(band_peers):
+            cells = pl.ds(pl.multiple_of(peer["band"] * share, share), share)
+            copies.append(send(src.at[:, cells], dst.at[mine], sems.at[0, i], sems.at[1, i], peer))
+    cells = pl.ds(pl.multiple_of(band * share, share), share)
+    for i, (src, dst) in enumerate(((field_ref, field), (image_ref, image))):
+        own = pltpu.make_async_copy(src.at[:, cells], dst.at[mine], own_sems.at[i])
+        own.start()
+        copies.append(own)
+    for copy in copies:
+        copy.wait()
+    total = jnp.zeros((2 * orbs, orbs), jnp.float32)
+    for row in range(0, share, 2):
+        right = jnp.concatenate([field[:, row, :], field[:, row + 1, :]], axis=1)
+        left = jnp.concatenate([image[:, row, :], image[:, row + 1, :]], axis=1)
+        total = total + contract(jnp.concatenate([right, left], axis=0), right)
+    total = jnp.concatenate([total, jnp.zeros((2 * orbs, lanes - orbs), jnp.float32)], axis=1)
+    for peer in range(bands):
+        for kind in range(2):
+            start = kind * orbs + peer * orb_dev
+            rows_out[peer, kind] = total[start : start + orb_dev]
+    rows_in[band] = rows_out[band]
+    copies = [
+        send(rows_out.at[peer["band"]], rows_in.at[band], row_sems.at[0, i], row_sems.at[1, i], peer)
+        for i, peer in enumerate(band_peers)
+    ]
+    for copy in copies:
+        copy.wait()
+    reduced = rows_in[0]
+    for i in range(1, bands):
+        reduced = reduced + rows_in[i]
+    part[...] = reduced
+    parts[domain] = reduced
+    copies = [
+        send(part, parts.at[domain], part_sems.at[0, i], part_sems.at[1, i], peer)
+        for i, peer in enumerate(domain_peers)
+    ]
+    for copy in copies:
+        copy.wait()
+    reduced = parts[0]
+    for i in range(1, domains):
+        reduced = reduced + parts[i]
+    reduced = reduced / cell_count
+    s_ref[...] = reduced[0, :, :orbs]
+    h_ref[...] = reduced[1, :, :orbs]
+
+
+def tiles(field, image, cell_count):
+    domains, bands = lax.axis_size("domain"), lax.axis_size("band")
+    orb_dev, rows, lanes = field.shape
+    orbs, share = orb_dev * bands, rows // bands
+    vmem = pl.BlockSpec(memory_space=pltpu.VMEM)
+    pair = (2, orb_dev, lanes)
+    gathered = pltpu.VMEM((orbs, share, lanes), jnp.float32)
+    return pl.pallas_call(
+        functools.partial(tiles_kernel, domains, bands, cell_count),
+        out_shape=[jax.ShapeDtypeStruct((orb_dev, orbs), jnp.float32)] * 2,
+        in_specs=[vmem] * 2,
+        out_specs=[vmem] * 2,
+        scratch_shapes=[
+            gathered,
+            gathered,
+            pltpu.VMEM((bands,) + pair, jnp.float32),
+            pltpu.VMEM((bands,) + pair, jnp.float32),
+            pltpu.VMEM(pair, jnp.float32),
+            pltpu.VMEM((domains,) + pair, jnp.float32),
+            pltpu.SemaphoreType.DMA((2, bands - 1)),
+            pltpu.SemaphoreType.DMA((2, bands - 1)),
+            pltpu.SemaphoreType.DMA((2,)),
+            pltpu.SemaphoreType.DMA((2, bands - 1)),
+            pltpu.SemaphoreType.DMA((2, domains - 1)),
+        ],
+        compiler_params=pltpu.CompilerParams(
+            collective_id=1, has_side_effects=True, vmem_limit_bytes=32 * 1024 * 1024
+        ),
+    )(field, image)
+
+
+def body_by_orbital(orbitals, potential):
+    orb_dev, planes, size_y, size_z = orbitals.shape
+    cell_count = planes * size_y * size_z * lax.axis_size("domain")
+    whole = lax.all_to_all(orbitals, "domain", split_axis=0, concat_axis=1, tiled=True)
+    filtered, image = filter_orbitals(whole, whole_potential(potential))
+    filtered = lax.all_to_all(filtered, "domain", split_axis=1, concat_axis=0, tiled=True)
+    image = lax.all_to_all(image, "domain", split_axis=1, concat_axis=0, tiled=True)
+    flat = (orb_dev, planes * size_y, size_z)
+    intersection, hamiltonian = tiles(filtered.reshape(flat), image.reshape(flat), cell_count)
+    return filtered, intersection, hamiltonian
+
+
+def body(orbitals, potential):
+    domains, bands = lax.axis_size("domain"), lax.axis_size("band")
+    orb_dev, planes, size_y, size_z = orbitals.shape
+    fits = (
+        orb_dev % domains == 0
+        and orb_dev % 8 == 0
+        and planes % stencil_reach == 0
+        and size_y % 16 == 0
+        and size_z == 128
+        and orb_dev * bands <= size_z
+        and (planes * size_y) % (8 * bands) == 0
+    )
+    if fits:
+        return body_by_orbital(orbitals, potential)
+    return body_by_block(orbitals, potential)
+
+
 def solution(mesh):
     placed = (P("band", "domain", None, None), P("domain", None, "band"))
     return jax.shard_map(

time: 602 us -> 197 us (0.33)
  waiting for transfers between devices: 434 us -> 56.3 us
  Pallas kernels: 0 us -> 119 us
  other arithmetic: 57.3 us -> 0 us
  blocking collectives: 43.6 us -> 0 us
  starting transfers between devices: 36.6 us -> 15.8 us
  between operations: 14.2 us -> 0.72 us
  matrix products: 9.91 us -> 0 us
    ppermute x18 -> x0, waiting for transfers between devices: 434 us -> none  [the longest x9 395 us: extended(): lax.ppermute(head, axis, [((i + 1) % count, i) for i in range(count)])]
    pallas_call x0 -> x3, Pallas kernels: none -> 119 us  [the longest x1 43 us: filter_orbitals(): pl.pallas_call(filter_kernel, out_shape=[jax.ShapeDtypeStruct(orbitals.sh...]
    all_to_all x0 -> x3, waiting for transfers between devices: none -> 56.3 us  [the longest x1 28.6 us: body_by_orbital(): lax.all_to_all(image, 'domain', split_axis=1, concat_axis=0, tiled=True)]
    sub x7 -> x0, other arithmetic: 44.5 us -> none  [body(): (apply_hamiltonian(current, local_pot) - centre * current) * (2.0 * sigma...]
    ppermute x18 -> x0, starting transfers between devices: 36.6 us -> none  [the longest x9 33.5 us: extended(): lax.ppermute(head, axis, [((i + 1) % count, i) for i in range(count)])]
    psum x1 -> x0, blocking collectives: 36.3 us -> none  [body(): s_total, h_total = lax.psum((s_part, h_part), 'domain')]
    all_to_all x0 -> x3, starting transfers between devices: none -> 15.8 us  [the longest x1 7.26 us: body_by_orbital(): lax.all_to_all(orbitals, 'domain', split_axis=0, concat_axis=1, tiled=True)]
    dot_general x2 -> x0, matrix products: 9.91 us -> none  [contract(): lax.dot_general(left, right, (((1,), (1,)), ((), ())), precision=lax.Prec...]
  transfers between devices with their start and end apart: 19 -> 3, of which waited for: 13 -> 2; matrix products, arithmetic and copies ran while one was open for 1% -> 1% of each run, Pallas kernels for 0% -> 19%
where the time goes in v1:
time: 197 us; the launch traced here: 196 us
  Pallas kernels  119 us (60%)
  waiting for transfers between devices  56.3 us (29%)
  starting transfers between devices  15.8 us (8%)
  local copies, waits for them, and re-layouts  4.65 us (2%)
    pallas_call x1, Pallas kernels, filter_orbitals(): pl.pallas_call(filter_kernel, out_shape=[jax.ShapeDtypeStruct(orbitals.sh...  43 us
    pallas_call x1, Pallas kernels, tiles(): pl.pallas_call(functools.partial(tiles_kernel, domains, bands, cell_count...  39.3 us
    pallas_call x1, Pallas kernels, whole_potential(): pl.pallas_call(functools.partial(potential_kernel, domains, bands), out_s...  36.7 us
    all_to_all x1, waiting for transfers between devices, body_by_orbital(): lax.all_to_all(image, 'domain', split_axis=1, concat_axis=0, tiled=True)  28.6 us
    all_to_all x1, waiting for transfers between devices, body_by_orbital(): lax.all_to_all(filtered, 'domain', split_axis=1, concat_axis=0, tiled=True)  27.7 us
    all_to_all x1, starting transfers between devices, body_by_orbital(): lax.all_to_all(orbitals, 'domain', split_axis=0, concat_axis=1, tiled=True)  7.26 us
    all_to_all x1, starting transfers between devices, body_by_orbital(): lax.all_to_all(filtered, 'domain', split_axis=1, concat_axis=0, tiled=True)  4.93 us
  transfers between devices with their start and end apart: 3, of which 2 were waited for; matrix products, arithmetic and copies ran while one was open for 1% of the time, Pallas kernels for 19%

profile of v1, /device:TPU:0, one launch (start us, length us, event | category | flops | bytes accessed | tf_op | source)
XLA Modules:
  0.0 196.4 jit_solution(12339067691976274899)
XLA Ops:
  0.6 7.3 %all-to-all-start = ((f32[24,6,16,128]{3,2,1,0:T(8,128)}), f32[24,6,16,128]{3,2,1,0:T(8,128)S(1)}, u32[]{:S(2)}, u32[]{:S(2)}) async-start(f32[24,6,16,128]{3,2,1,0:T(8,128)} %param.3), calls=%async_computation | async-start | bytes 2359296 | tf_op jit(solution)/shard_map/all_to_all | solution.py:430
  7.9 36.7 %shard_map.58.pot_ref = f32[48,16,128]{2,1,0:T(8,128)} custom-call(f32[6,16,32]{2,1,0:T(8,128)} %part_ref.1), custom_call_target="tpu_custom_call" | custom-call | tf_op jit(solution)/shard_map/pallas_call | solution.py:322
  44.6 0.0 all-to-all-done
  44.6 0.0 copy-start.1
  44.6 0.0 copy-start.2
  44.7 0.1 copy.9
  44.8 0.9 copy-done.1
  45.6 0.0 copy-done.2
  45.7 43.0 %shard_map.59 = (f32[3,48,16,128]{3,2,1,0:T(8,128)S(1)}, f32[3,48,16,128]{3,2,1,0:T(8,128)S(1)}) custom-call(f32[3,48,16,128]{3,2,1,0:T(8,128)S(1)} %bitcast.16, f32[48,16,128]{2,1,0:T(8,128)S(1)} %copy-done.1, bf16[256,384]{1,0:T(8,128)(2,1)S(1)} %copy-done.2), custom_call_target="tpu_custom_call" | custom-call | tf_op jit(solution)/shard_map/pallas_call | solution.py:253
  88.6 1.1 copy.10
  89.7 4.9 %all-to-all-start.1 = ((f32[3,48,16,128]{3,2,0,1:T(8,128)}), f32[3,48,16,128]{3,2,0,1:T(8,128)S(1)}, u32[]{:S(2)}, u32[]{:S(2)}) async-start(f32[3,48,16,128]{3,2,0,1:T(8,128)} %copy.10), calls=%async_computation.1 | async-start | bytes 2359296 | tf_op jit(solution)/shard_map/all_to_all | solution.py:432
  94.7 1.1 copy.12
  95.8 27.7 %all-to-all-done.1 = f32[3,48,16,128]{3,2,0,1:T(8,128)S(1)} async-done(((f32[3,48,16,128]{3,2,0,1:T(8,128)}), f32[3,48,16,128]{3,2,0,1:T(8,128)S(1)}, u32[]{:S(2)}, u32[]{:S(2)}) %all-to-all-start.1) | async-done | bytes 1179680 | tf_op jit(solution)/shard_map/all_to_all | solution.py:432
  123.4 3.6 %all-to-all-start.2 = ((f32[3,48,16,128]{3,2,0,1:T(8,128)}), f32[3,48,16,128]{3,2,0,1:T(8,128)S(1)}, u32[]{:S(2)}, u32[]{:S(2)}) async-start(f32[3,48,16,128]{3,2,0,1:T(8,128)} %copy.12), calls=%async_computation.2 | async-start | bytes 2359296 | tf_op jit(solution)/shard_map/all_to_all | solution.py:433
  127.1 0.1 copy.11
  127.2 0.0 copy-start
  127.2 28.6 %all-to-all-done.2 = f32[3,48,16,128]{3,2,0,1:T(8,128)S(1)} async-done(((f32[3,48,16,128]{3,2,0,1:T(8,128)}), f32[3,48,16,128]{3,2,0,1:T(8,128)S(1)}, u32[]{:S(2)}, u32[]{:S(2)}) %all-to-all-start.2) | async-done | bytes 1179680 | tf_op jit(solution)/shard_map/all_to_all | solution.py:433
  155.8 0.1 copy.13
  155.9 0.0 copy-done
  155.9 39.3 %shard_map.60 = (f32[24,96]{1,0:T(8,128)S(1)}, f32[24,96]{1,0:T(8,128)S(1)}) custom-call(f32[24,96,128]{2,1,0:T(8,128)S(1)} %bitcast.14, f32[24,96,128]{2,1,0:T(8,128)S(1)} %bitcast.17), custom_call_target="tpu_custom_call" | custom-call | tf_op jit(solution)/shard_map/pallas_call | solution.py:403
  195.2 0.6 copy.16
  195.8 0.6 copy.17
Async XLA Ops:
  0.6 44.0 %all-to-all-start = ((f32[24,6,16,128]{3,2,1,0:T(8,128)}), f32[24,6,16,128]{3,2,1,0:T(8,128)S(1)}, u32[]{:S(2)}, u32[]{:S(2)}) async-start(f32[24,6,16,128]{3,2,1,0:T(8,128)} %param.3), calls=%async_computation | async-start | bytes 2359296 | tf_op jit(solution)/shard_map/all_to_all | solution.py:430
  44.6 1.0 copy-start.1
  44.6 1.0 copy-start.2
  89.7 33.7 %all-to-all-start.1 = ((f32[3,48,16,128]{3,2,0,1:T(8,128)}), f32[3,48,16,128]{3,2,0,1:T(8,128)S(1)}, u32[]{:S(2)}, u32[]{:S(2)}) async-start(f32[3,48,16,128]{3,2,0,1:T(8,128)} %copy.10), calls=%async_computation.1 | async-start | bytes 2359296 | tf_op jit(solution)/shard_map/all_to_all | solution.py:432
  123.4 32.4 %all-to-all-start.2 = ((f32[3,48,16,128]{3,2,0,1:T(8,128)}), f32[3,48,16,128]{3,2,0,1:T(8,128)S(1)}, u32[]{:S(2)}, u32[]{:S(2)}) async-start(f32[3,48,16,128]{3,2,0,1:T(8,128)} %copy.12), calls=%async_computation.2 | async-start | bytes 2359296 | tf_op jit(solution)/shard_map/all_to_all | solution.py:433
  127.2 28.8 %copy-start = (f32[3,8,6,16,128]{4,3,2,0,1:T(8,128)}, f32[3,8,6,16,128]{4,3,2,0,1:T(8,128)S(1)}, u32[]{:S(2)}) copy-start(f32[3,8,6,16,128]{4,3,2,0,1:T(8,128)S(1)} %copy.11) | copy-start | bytes 3538948

commit v2 on v1

--- a/solution.py
+++ b/solution.py
@@ -202,64 +202,6 @@
     return results
 
 
-def filter_kernel(orb_ref, pot_ref, weight_ref, out_ref, image_ref, first, second, shifted_pot):
-    count, size_x, size_y, size_z = orb_ref.shape
-    reach = stencil_reach
-    groups = size_x // reach
-    centre, steps = schedule()
-    weights = weight_ref[...]
-    shifted_pot[...] = pot_ref[...] + (-1.5 * stencil_coeffs[0] - centre)
-    zeros = jnp.zeros((size_x, pad_rows, size_z), jnp.float32)
-    for buf in (first, second):
-        buf[:, pl.ds(0, pad_rows), :] = zeros
-        buf[:, pl.ds(pad_rows + size_y, pad_rows), :] = zeros
-    inner = pl.ds(pad_rows, size_y)
-
-    def one_orbital(orb, carry):
-        first[:, inner, :] = orb_ref[orb]
-        buffers = [first, second]
-        for scale, back in steps:
-            src, dst = buffers
-
-            def one_group(group, carry, src=src, dst=dst, scale=scale, back=back):
-                for i, total in enumerate(shifted_h(src, group, groups, shifted_pot, weights)):
-                    update = total * scale
-                    if back:
-                        update = update - back * dst[group * reach + i, inner, :]
-                    dst[group * reach + i, inner, :] = update
-                return carry
-
-            lax.fori_loop(0, groups, one_group, 0)
-            buffers = [dst, src]
-        src = buffers[0]
-
-        def image_group(group, carry):
-            for i, total in enumerate(shifted_h(src, group, groups, shifted_pot, weights)):
-                cells = src[group * reach + i, inner, :]
-                out_ref[orb, group * reach + i] = cells
-                image_ref[orb, group * reach + i] = total + centre * cells
-            return carry
-
-        lax.fori_loop(0, groups, image_group, 0)
-        return carry
-
-    lax.fori_loop(0, count, one_orbital, 0)
-
-
-def filter_orbitals(orbitals, potential):
-    count, size_x, size_y, size_z = orbitals.shape
-    vmem = pl.BlockSpec(memory_space=pltpu.VMEM)
-    padded = pltpu.VMEM((size_x, size_y + 2 * pad_rows, size_z), jnp.float32)
-    return pl.pallas_call(
-        filter_kernel,
-        out_shape=[jax.ShapeDtypeStruct(orbitals.shape, jnp.float32)] * 2,
-        in_specs=[vmem] * 3,
-        out_specs=[vmem] * 2,
-        scratch_shapes=[padded, padded, pltpu.VMEM((size_x, size_y, size_z), jnp.float32)],
-        compiler_params=pltpu.CompilerParams(vmem_limit_bytes=32 * 1024 * 1024),
-    )(orbitals, potential, jnp.asarray(band_matrix(size_z)))
-
-
 def greet(peers):
     barrier = pltpu.get_barrier_semaphore()
     for peer in peers:
@@ -285,53 +227,142 @@
     return copy
 
 
-def potential_kernel(domains, bands, part_ref, out_ref, by_band, whole, band_sems, domain_sems):
-    planes, size_y, part = part_ref.shape
+def filter_kernel(
+    domains, bands, orb_ref, part_ref, weight_ref, out_ref, image_ref,
+    whole_orb, field, image, by_band, whole_pot, first, second,
+    band_sems, domain_sems, in_sems, field_sems, image_sems,
+):
+    count, size_x, size_y, size_z = whole_orb.shape
+    planes, _, part = part_ref.shape
+    reach = stencil_reach
+    groups = size_x // reach
+    centre, steps = schedule()
     band, domain = lax.axis_index("band"), lax.axis_index("domain")
     band_peers, domain_peers = others("band", bands), others("domain", domains)
     greet(band_peers + domain_peers)
+    block = pl.ds(domain * planes, planes)
+
+    def send_orbital(orb):
+        return [
+            send(
+                orb_ref.at[peer["domain"] * count + orb],
+                whole_orb.at[orb, block],
+                in_sems.at[0, orb, i],
+                in_sems.at[1, orb, i],
+                peer,
+            )
+            for i, peer in enumerate(domain_peers)
+        ]
+
+    def send_result(src, dst, sems, orb):
+        return [
+            send(
+                src.at[orb, pl.ds(peer["domain"] * planes, planes)],
+                dst.at[domain * count + orb],
+                sems.at[0, orb, i],
+                sems.at[1, orb, i],
+                peer,
+            )
+            for i, peer in enumerate(domain_peers)
+        ]
+
     spread = jnp.concatenate([part_ref[...]] * bands, axis=2)
     lane = lax.broadcasted_iota(jnp.int32, spread.shape, 2)
     mine = (lane >= band * part) & (lane < (band + 1) * part)
     by_band[band] = jnp.where(mine, spread, 0.0)
-    copies = [
+    band_copies = [
         send(by_band.at[band], by_band.at[band], band_sems.at[0, i], band_sems.at[1, i], peer)
         for i, peer in enumerate(band_peers)
     ]
-    for copy in copies:
+    arriving = [send_orbital(0)]
+    for copy in band_copies:
         copy.wait()
     total = by_band[0]
     for i in range(1, bands):
         total = total + by_band[i]
-    block = pl.ds(domain * planes, planes)
-    whole[block] = total
-    copies = [
-        send(whole.at[block], whole.at[block], domain_sems.at[0, i], domain_sems.at[1, i], peer)
+    whole_pot[block] = total + (-1.5 * stencil_coeffs[0] - centre)
+    pot_copies = [
+        send(whole_pot.at[block], whole_pot.at[block], domain_sems.at[0, i], domain_sems.at[1, i], peer)
         for i, peer in enumerate(domain_peers)
     ]
-    for copy in copies:
-        copy.wait()
-    out_ref[...] = whole[...]
-
-
-def whole_potential(potential):
+    arriving += [send_orbital(orb) for orb in range(1, count)]
+    for orb in range(count):
+        whole_orb[orb, block] = orb_ref[domain * count + orb]
+    zeros = jnp.zeros((size_x, pad_rows, size_z), jnp.float32)
+    for buf in (first, second):
+        buf[:, pl.ds(0, pad_rows), :] = zeros
+        buf[:, pl.ds(pad_rows + size_y, pad_rows), :] = zeros
+    weights = weight_ref[...]
+    inner = pl.ds(pad_rows, size_y)
+    for copy in pot_copies:
+        copy.wait()
+    leaving = []
+    for orb in range(count):
+        for copy in arriving[orb]:
+            copy.wait()
+        first[:, inner, :] = whole_orb[orb]
+        buffers = [first, second]
+        for scale, back in steps:
+            src, dst = buffers
+
+            def one_group(group, carry, src=src, dst=dst, scale=scale, back=back):
+                for i, total in enumerate(shifted_h(src, group, groups, whole_pot, weights)):
+                    update = total * scale
+                    if back:
+                        update = update - back * dst[group * reach + i, inner, :]
+                    dst[group * reach + i, inner, :] = update
+                return carry
+
+            lax.fori_loop(0, groups, one_group, 0)
+            buffers = [dst, src]
+        src = buffers[0]
+        field[orb] = src[:, inner, :]
+        leaving += send_result(field, out_ref, field_sems, orb)
+
+        def image_group(group, carry, src=src, orb=orb):
+            for i, total in enumerate(shifted_h(src, group, groups, whole_pot, weights)):
+                image[orb, group * reach + i] = total + centre * src[group * reach + i, inner, :]
+            return carry
+
+        lax.fori_loop(0, groups, image_group, 0)
+        leaving += send_result(image, image_ref, image_sems, orb)
+        out_ref[domain * count + orb] = field[orb, block]
+        image_ref[domain * count + orb] = image[orb, block]
+    for copy in leaving:
+        copy.wait()
+
+
+def filter_orbitals(orbitals, potential):
     domains, bands = lax.axis_size("domain"), lax.axis_size("band")
-    planes, size_y, part = potential.shape
+    orb_dev, planes, size_y, size_z = orbitals.shape
+    count, size_x = orb_dev // domains, planes * domains
     vmem = pl.BlockSpec(memory_space=pltpu.VMEM)
-    whole = (domains * planes, size_y, bands * part)
+    whole = pltpu.VMEM((count, size_x, size_y, size_z), jnp.float32)
+    padded = pltpu.VMEM((size_x, size_y + 2 * pad_rows, size_z), jnp.float32)
+    by_orbital = pltpu.SemaphoreType.DMA((2, count, domains - 1))
     return pl.pallas_call(
-        functools.partial(potential_kernel, domains, bands),
-        out_shape=jax.ShapeDtypeStruct(whole, jnp.float32),
-        in_specs=[vmem],
-        out_specs=vmem,
+        functools.partial(filter_kernel, domains, bands),
+        out_shape=[jax.ShapeDtypeStruct(orbitals.shape, jnp.float32)] * 2,
+        in_specs=[vmem] * 3,
+        out_specs=[vmem] * 2,
         scratch_shapes=[
-            pltpu.VMEM((bands, planes, size_y, bands * part), jnp.float32),
-            pltpu.VMEM(whole, jnp.float32),
+            whole,
+            whole,
+            whole,
+            pltpu.VMEM((bands, planes, size_y, size_z), jnp.float32),
+            pltpu.VMEM((size_x, size_y, size_z), jnp.float32),
+            padded,
+            padded,
             pltpu.SemaphoreType.DMA((2, bands - 1)),
             pltpu.SemaphoreType.DMA((2, domains - 1)),
+            by_orbital,
+            by_orbital,
+            by_orbital,
         ],
-        compiler_params=pltpu.CompilerParams(collective_id=0, has_side_effects=True),
-    )(potential)
+        compiler_params=pltpu.CompilerParams(
+            collective_id=0, has_side_effects=True, vmem_limit_bytes=40 * 1024 * 1024
+        ),
+    )(orbitals, potential, jnp.asarray(band_matrix(size_z)))
 
 
 def tiles_kernel(
@@ -427,10 +458,7 @@
 def body_by_orbital(orbitals, potential):
     orb_dev, planes, size_y, size_z = orbitals.shape
     cell_count = planes * size_y * size_z * lax.axis_size("domain")
-    whole = lax.all_to_all(orbitals, "domain", split_axis=0, concat_axis=1, tiled=True)
-    filtered, image = filter_orbitals(whole, whole_potential(potential))
-    filtered = lax.all_to_all(filtered, "domain", split_axis=1, concat_axis=0, tiled=True)
-    image = lax.all_to_all(image, "domain", split_axis=1, concat_axis=0, tiled=True)
+    filtered, image = filter_orbitals(orbitals, potential)
     flat = (orb_dev, planes * size_y, size_z)
     intersection, hamiltonian = tiles(filtered.reshape(flat), image.reshape(flat), cell_count)
     return filtered, intersection, hamiltonian

time: 197 us -> 142 us (0.72)
  waiting for transfers between devices: 56.3 us -> 0 us
  Pallas kernels: 119 us -> 136 us
  starting transfers between devices: 15.8 us -> 0 us
    all_to_all x3 -> x0, waiting for transfers between devices: 56.3 us -> none  [the longest x1 28.6 us: body_by_orbital(): lax.all_to_all(image, 'domain', split_axis=1, concat_axis=0, tiled=True)]
    all_to_all x3 -> x0, starting transfers between devices: 15.8 us -> none  [the longest x1 7.26 us: body_by_orbital(): lax.all_to_all(orbitals, 'domain', split_axis=0, concat_axis=1, tiled=True)]
    pallas_call x2 -> x1, Pallas kernels: 79.7 us -> 92.5 us  [filter_orbitals(): pl.pallas_call(functools.partial(filter_kernel, domains, bands), out_shap...]
    pallas_call x1, Pallas kernels: 39.3 us -> 43.3 us  [tiles(): pl.pallas_call(functools.partial(tiles_kernel, domains, bands, cell_count...]
    unnamed x8 -> x9, local copies, waits for them, and re-layouts: 2.14 us -> 5.2 us
    pallas_call x2 -> x0, local copies, waits for them, and re-layouts: 2.19 us -> none  [filter_orbitals(): pl.pallas_call(filter_kernel, out_shape=[jax.ShapeDtypeStruct(orbitals.sh...]
  transfers between devices with their start and end apart: 3 -> 0, of which waited for: 2 -> 0; matrix products, arithmetic and copies ran while one was open for 1% -> 0% of each run, Pallas kernels for 19% -> 0%
where the time goes in v2:
time: 142 us
  Pallas kernels  136 us (96%)
  local copies, waits for them, and re-layouts  5.2 us (4%)
    pallas_call x1, Pallas kernels, filter_orbitals(): pl.pallas_call(functools.partial(filter_kernel, domains, bands), out_shap...  92.5 us
    pallas_call x1, Pallas kernels, tiles(): pl.pallas_call(functools.partial(tiles_kernel, domains, bands, cell_count...  43.3 us
    unnamed x9, local copies, waits for them, and re-layouts  5.2 us

profile of v2, /device:TPU:0, one launch (start us, length us, event | category | flops | bytes accessed | tf_op | source)
XLA Modules:
  0.0 141.7 jit_solution(13749643480862916298)
XLA Ops:
  0.6 0.0 copy-start
  0.6 1.3 copy-done
  1.9 0.0 copy-start.1
  1.9 0.9 copy-done.1
  2.8 0.0 copy-start.2
  2.8 0.8 copy-done.2
  3.6 92.5 %shard_map.58 = (f32[24,6,16,128]{3,2,1,0:T(8,128)S(1)}, f32[24,6,16,128]{3,2,1,0:T(8,128)S(1)}) custom-call(f32[24,6,16,128]{3,2,1,0:T(8,128)S(1)} %copy-done, f32[6,16,32]{2,1,0:T(8,128)S(1)} %copy-done.2, bf16[256,384]{1,0:T(8,128)(2,1)S(1)} %copy-done.1), custom_call_target="tpu_custom_call" | custom-call | tf_op jit(solution)/shard_map/pallas_call | solution.py:343
  96.2 43.3 %shard_map.59 = (f32[24,96]{1,0:T(8,128)S(1)}, f32[24,96]{1,0:T(8,128)S(1)}) custom-call(f32[24,96,128]{2,1,0:T(8,128)S(1)} %bitcast.2, f32[24,96,128]{2,1,0:T(8,128)S(1)} %bitcast.3), custom_call_target="tpu_custom_call" | custom-call | tf_op jit(solution)/shard_map/pallas_call | solution.py:434
  139.4 1.0 copy.9
  140.5 0.6 copy.10
  141.1 0.6 copy.11
Async XLA Ops:
  0.6 1.3 copy-start
  1.9 0.9 copy-start.1
  2.8 0.8 copy-start.2

commit v3 on v2

--- a/solution.py
+++ b/solution.py
@@ -376,23 +376,32 @@
     band_peers, domain_peers = others("band", bands), others("domain", domains)
     greet(band_peers + domain_peers)
     mine = pl.ds(pl.multiple_of(band * orb_dev, orb_dev), orb_dev)
-    copies = []
-    for src, dst, sems in ((field_ref, field, field_sems), (image_ref, image, image_sems)):
+    own_cells = pl.ds(pl.multiple_of(band * share, share), share)
+    pending = []
+    for kind, (src, dst, sems) in enumerate(
+        ((field_ref, field, field_sems), (image_ref, image, image_sems))
+    ):
+        copies = []
         for i, peer in enumerate(band_peers):
             cells = pl.ds(pl.multiple_of(peer["band"] * share, share), share)
             copies.append(send(src.at[:, cells], dst.at[mine], sems.at[0, i], sems.at[1, i], peer))
-    cells = pl.ds(pl.multiple_of(band * share, share), share)
-    for i, (src, dst) in enumerate(((field_ref, field), (image_ref, image))):
-        own = pltpu.make_async_copy(src.at[:, cells], dst.at[mine], own_sems.at[i])
+        own = pltpu.make_async_copy(src.at[:, own_cells], dst.at[mine], own_sems.at[kind])
         own.start()
-        copies.append(own)
-    for copy in copies:
-        copy.wait()
-    total = jnp.zeros((2 * orbs, orbs), jnp.float32)
+        pending.append(copies + [own])
+    for copy in pending[0]:
+        copy.wait()
+    rights = []
+    s_total = jnp.zeros((orbs, orbs), jnp.float32)
     for row in range(0, share, 2):
-        right = jnp.concatenate([field[:, row, :], field[:, row + 1, :]], axis=1)
+        rights.append(jnp.concatenate([field[:, row, :], field[:, row + 1, :]], axis=1))
+        s_total = s_total + contract(rights[-1], rights[-1])
+    for copy in pending[1]:
+        copy.wait()
+    h_total = jnp.zeros((orbs, orbs), jnp.float32)
+    for row in range(0, share, 2):
         left = jnp.concatenate([image[:, row, :], image[:, row + 1, :]], axis=1)
-        total = total + contract(jnp.concatenate([right, left], axis=0), right)
+        h_total = h_total + contract(left, rights[row // 2])
+    total = jnp.concatenate([s_total, h_total], axis=0)
     total = jnp.concatenate([total, jnp.zeros((2 * orbs, lanes - orbs), jnp.float32)], axis=1)
     for peer in range(bands):
         for kind in range(2):

time: 142 us -> 141 us (level)
  no operation moved by 1% of the time
where the time goes in v3:
time: 141 us
  Pallas kernels  135 us (96%)
  local copies, waits for them, and re-layouts  5.2 us (4%)
    pallas_call x1, Pallas kernels, filter_orbitals(): pl.pallas_call(functools.partial(filter_kernel, domains, bands), out_shap...  92.5 us
    pallas_call x1, Pallas kernels, tiles(): pl.pallas_call(functools.partial(tiles_kernel, domains, bands, cell_count...  42.4 us
    unnamed x9, local copies, waits for them, and re-layouts  5.2 us

profile of v3, /device:TPU:0, one launch (start us, length us, event | category | flops | bytes accessed | tf_op | source)
XLA Modules:
  0.0 140.8 jit_solution(5436930797134899017)
XLA Ops:
  0.6 0.0 copy-start
  0.6 1.3 copy-done
  1.9 0.0 copy-start.1
  1.9 0.9 copy-done.1
  2.8 0.0 copy-start.2
  2.8 0.8 copy-done.2
  3.6 92.5 %shard_map.58 = (f32[24,6,16,128]{3,2,1,0:T(8,128)S(1)}, f32[24,6,16,128]{3,2,1,0:T(8,128)S(1)}) custom-call(f32[24,6,16,128]{3,2,1,0:T(8,128)S(1)} %copy-done, f32[6,16,32]{2,1,0:T(8,128)S(1)} %copy-done.2, bf16[256,384]{1,0:T(8,128)(2,1)S(1)} %copy-done.1), custom_call_target="tpu_custom_call" | custom-call | tf_op jit(solution)/shard_map/pallas_call | solution.py:343
  96.2 42.4 %shard_map.59 = (f32[24,96]{1,0:T(8,128)S(1)}, f32[24,96]{1,0:T(8,128)S(1)}) custom-call(f32[24,96,128]{2,1,0:T(8,128)S(1)} %bitcast.2, f32[24,96,128]{2,1,0:T(8,128)S(1)} %bitcast.3), custom_call_target="tpu_custom_call" | custom-call | tf_op jit(solution)/shard_map/pallas_call | solution.py:443
  138.6 1.0 copy.9
  139.6 0.6 copy.10
  140.2 0.6 copy.11
Async XLA Ops:
  0.6 1.3 copy-start
  1.9 0.9 copy-start.1
  2.8 0.8 copy-start.2
